TPU v7x, 32 devices: a whole 2x2x4 slice. The times are simulated.
32 devices in a mesh: branch: 4 (over y, x), row: 8 (over z, core).
Axes of the slice: x: 2, y: 2, z: 4, core: 2. Of those that a mesh axis runs over, the one named last changes fastest.
Arguments:
- root_cov: bfloat16 [2304, 2304], P('row', 'branch')
- diag_factor: float32 [4, 3, 576, 576], P('branch')
- panel_factor: float32 [4, 3, 2304, 576], P('branch', None, 'row'), may hold values from -0.009765625 to 0.009765625
- chain_factor: float32 [4, 2, 576, 576], P('branch'), may hold values from -0.25 to 0.25
- panel_tiles: int32 [4, 3], P('branch'), may hold values from 0 to 3, as said below
Outputs:
- panel_cov: float32 [4, 3, 2304, 576], P('branch', None, 'row')
- block_cov: float32 [4, 5, 576, 576], P('branch')
Inputs may be any that keep to these rules, and one draw needn't show every extreme that they name: `panel_tiles`: the entries of a row are distinct; the first 2 and the first 1 entries of a row are the level-two and level-three patterns.
All inputs are finite; a program needn't handle non-finite values.
Results may differ from a plain program's by a relative error of at most 0.0029.
Values may be sent and summed in bfloat16 or wider, within the bound.
A program may use at most 192 MiB of HBM per device.

v0:
```python
import functools
import jax
import jax.numpy as jnp
from jax import lax
from jax.experimental import pallas as pl
from jax.experimental.pallas import tpu as pltpu
from jax.sharding import PartitionSpec as P

BF = jnp.bfloat16
F32 = jnp.float32
MESH = pl.DeviceIdType.MESH


def product(left_mat, right_mat):
    return jnp.dot(left_mat, right_mat, precision=lax.Precision.HIGH, preferred_element_type=F32)


def split(x):
    hi = x.astype(BF)
    return hi, (x - hi.astype(F32)).astype(BF)


def mm(a, b):
    return jnp.dot(a, b, preferred_element_type=F32)


def dot3(a, b):
    a_hi, a_lo = a
    b_hi, b_lo = b
    return mm(a_hi, b_hi) + (mm(a_lo, b_hi) + mm(a_hi, b_lo))


def inverse_kernel(size, window, l_ref, out_ref):
    count = size // window
    row = lax.broadcasted_iota(jnp.int32, (window, window), 0)
    col = lax.broadcasted_iota(jnp.int32, (window, window), 1)
    eye = row == col
    diagonals = []
    for w in range(count):
        at = slice(w * window, (w + 1) * window)
        block = l_ref[0, 0, at, at]
        kept = jnp.where(eye, block, 0.0)
        down = 1.0 / jnp.sum(kept, axis=1, keepdims=True)
        across = 1.0 / jnp.sum(kept, axis=0, keepdims=True)
        diagonals.append((block * down, across))
    found = []
    for scaled, across in diagonals:
        x = jnp.where(eye, 1.0, 0.0)
        x = x - jnp.where((row // 2 == col // 2) & (row > col), scaled, 0.0)
        found.append(x)
    k = 2
    while k < window:
        pair = (row // (2 * k) == col // (2 * k)) & (row // k > col // k)
        for w in range(count):
            x = found[w]
            parts = split(x)
            right = dot3(split(jnp.where(pair, diagonals[w][0], 0.0)), parts)
            found[w] = x - dot3(parts, split(right))
        k *= 2
    found = [x * diagonals[w][1] for w, x in enumerate(found)]
    done = {}
    for w in range(count):
        done[w, w] = split(found[w])
        out_ref[0, w * window:(w + 1) * window, w * window:(w + 1) * window] = found[w]
    for gap in range(1, count):
        for c in range(count - gap):
            r = c + gap
            total = None
            for m in range(c, r):
                below = split(l_ref[0, 0, r * window:(r + 1) * window, m * window:(m + 1) * window])
                term = dot3(below, done[m, c])
                total = term if total is None else total + term
            value = -dot3(done[r, r], split(total))
            done[r, c] = split(value)
            out_ref[0, r * window:(r + 1) * window, c * window:(c + 1) * window] = value
            out_ref[0, c * window:(c + 1) * window, r * window:(r + 1) * window] = jnp.zeros(
                (window, window), F32
            )


def inverses(diag_factor):
    levels, size = diag_factor.shape[1], diag_factor.shape[-1]
    return pl.pallas_call(
        functools.partial(inverse_kernel, size, size // 3),
        grid=(levels,),
        in_specs=[pl.BlockSpec((1, 1, size, size), lambda i: (0, i, 0, 0))],
        out_specs=pl.BlockSpec((1, size, size), lambda i: (i, 0, 0)),
        out_shape=jax.ShapeDtypeStruct((levels, size, size), F32),
        compiler_params=pltpu.CompilerParams(vmem_limit_bytes=48 * 2**20),
        name="inverses",
    )(diag_factor)


def sum_kernel(x_ref, out_ref, pair, send, landed, right_got, left_got, right_sib, left_sib, final,
               final_sib, pair_s, pair_r, rs_s, rs_r, right_s, right_r, left_s, left_r, sib_s, sib_r):
    me = lax.axis_index("row")
    z = me // 2
    core = me % 2
    sibling = 2 * z + 1 - core

    def at_chip(chip):
        return {"row": 2 * chip + core}

    barrier = pltpu.get_barrier_semaphore()
    pl.semaphore_signal(barrier, inc=1, device_id={"row": sibling}, device_id_type=MESH)
    for k in (1, 2, 3):
        pl.semaphore_signal(
            barrier, inc=1, device_id=at_chip((z + k) % 4), device_id_type=MESH
        )
    pl.semaphore_wait(barrier, 4)

    def copy(src, dst, send_sem, recv_sem, target):
        return pltpu.make_async_remote_copy(
            src_ref=src, dst_ref=dst, send_sem=send_sem, recv_sem=recv_sem,
            device_id=target, device_id_type=MESH,
        )

    to_pair = {}
    for k in (2, 1, 3, 0):
        to_pair[k] = copy(
            x_ref.at[1 - core, (z + k) % 4], pair.at[k], pair_s.at[k], pair_r.at[k],
            {"row": sibling},
        )
        to_pair[k].start()
    scatter = {}
    for k in (2, 1, 3):
        to_pair[k].wait_recv()
        send[k - 1] = (x_ref[core, (z + k) % 4] + pair[k]).astype(BF)
        scatter[k] = copy(
            send.at[k - 1], landed.at[k - 1], rs_s.at[k - 1], rs_r.at[k - 1],
            at_chip((z + k) % 4),
        )
        scatter[k].start()
    to_pair[0].wait_recv()
    pair[0] = pair[0] + x_ref[core, z]
    for k in (1, 3, 2):
        scatter[k].wait_recv()
        pair[0] = pair[0] + landed[k - 1].astype(F32)
    final[...] = pair[0].astype(BF)

    rights, lefts, sibs = {}, {}, {}
    sibs[0] = copy(final, final_sib, sib_s.at[0], sib_r.at[0], {"row": sibling})
    for s in (1, 2, 3):
        rights[s] = copy(
            final if s == 1 else right_got.at[s - 2], right_got.at[s - 1],
            right_s.at[s - 1], right_r.at[s - 1], at_chip(jnp.minimum(z + 1, 3)),
        )
        lefts[s] = copy(
            final if s == 1 else left_got.at[s - 2], left_got.at[s - 1],
            left_s.at[s - 1], left_r.at[s - 1], at_chip(jnp.maximum(z - 1, 0)),
        )
        sibs[s] = copy(
            right_got.at[s - 1], right_sib.at[s - 1], sib_s.at[s], sib_r.at[s], {"row": sibling}
        )
        sibs[-s] = copy(
            left_got.at[s - 1], left_sib.at[s - 1], sib_s.at[3 + s], sib_r.at[3 + s],
            {"row": sibling},
        )

    def goes_right(s):
        return (z < 3) & (z >= s - 1)

    def goes_left(s):
        return (z > 0) & (z + s <= 4)

    pl.when(goes_right(1))(rights[1].start)
    pl.when(goes_left(1))(lefts[1].start)
    sibs[0].start()
    out_ref[core, z] = final[...].astype(F32)
    for s in (1, 2, 3):
        @pl.when(z >= s)
        def _():
            rights[s].wait_recv()
            sibs[s].start()

        if s < 3:
            pl.when(goes_right(s + 1))(rights[s + 1].start)

        @pl.when(z + s <= 3)
        def _():
            lefts[s].wait_recv()
            sibs[-s].start()

        if s < 3:
            pl.when(goes_left(s + 1))(lefts[s + 1].start)

        @pl.when(z >= s)
        def _():
            out_ref[core, z - s] = right_got[s - 1].astype(F32)

        @pl.when(z + s <= 3)
        def _():
            out_ref[core, z + s] = left_got[s - 1].astype(F32)

    sibs[0].wait_recv()
    out_ref[1 - core, z] = final_sib[...].astype(F32)
    for s in (1, 2, 3):
        @pl.when(z >= s)
        def _():
            sibs[s].wait_recv()
            out_ref[1 - core, z - s] = right_sib[s - 1].astype(F32)

        @pl.when(z + s <= 3)
        def _():
            sibs[-s].wait_recv()
            out_ref[1 - core, z + s] = left_sib[s - 1].astype(F32)

    for k in (0, 1, 2, 3):
        to_pair[k].wait_send()
        if k:
            scatter[k].wait_send()
    sibs[0].wait_send()
    for s in (1, 2, 3):
        pl.when(goes_right(s))(rights[s].wait_send)
        pl.when(goes_left(s))(lefts[s].wait_send)
        pl.when(z >= s)(sibs[s].wait_send)
        pl.when(z + s <= 3)(sibs[-s].wait_send)


def line_sum(x, total):
    rows, columns = x.shape[0] // 8, x.shape[1]
    dma = pltpu.SemaphoreType.DMA
    whole = pl.BlockSpec(memory_space=pltpu.VMEM)
    out = pl.pallas_call(
        sum_kernel,
        out_shape=jax.ShapeDtypeStruct((2, 4, rows, columns), F32),
        in_specs=[whole],
        out_specs=whole,
        scratch_shapes=[
            pltpu.VMEM((4, rows, columns), F32),
            *[pltpu.VMEM((3, rows, columns), BF) for _ in range(6)],
            pltpu.VMEM((rows, columns), BF),
            pltpu.VMEM((rows, columns), BF),
            dma((4,)), dma((4,)),
            *[dma((3,)) for _ in range(6)],
            dma((7,)), dma((7,)),
        ],
        compiler_params=pltpu.CompilerParams(
            collective_id=0, has_side_effects=True, vmem_limit_bytes=48 * 2**20
        ),
        name="line_sum",
    )(x.reshape(2, 4, rows, columns))
    return out.reshape(8 * rows, columns)[:total]


def gather_kernel(x_ref, out_ref, right_s, right_r, left_s, left_r, sib_s, sib_r, own_s):
    me = lax.axis_index("row")
    z = me // 2
    core = me % 2
    sibling = 2 * z + 1 - core
    right = 2 * jnp.minimum(z + 1, 3) + core
    left = 2 * jnp.maximum(z - 1, 0) + core
    barrier = pltpu.get_barrier_semaphore()
    pl.semaphore_signal(barrier, inc=1, device_id={"row": sibling}, device_id_type=MESH)
    for k in (1, 2, 3):
        pl.semaphore_signal(
            barrier, inc=1, device_id={"row": 2 * ((z + k) % 4) + core}, device_id_type=MESH
        )
    pl.semaphore_wait(barrier, 4)

    def moved(source, part, send_sem, recv_sem, target, first):
        return pltpu.make_async_remote_copy(
            src_ref=x_ref.at[part] if first else out_ref.at[source, part],
            dst_ref=out_ref.at[source, part], send_sem=send_sem, recv_sem=recv_sem,
            device_id={"row": target}, device_id_type=MESH,
        )

    steps = [(s, p) for s in (1, 2, 3) for p in (0, 1)]
    rights, lefts, sib_right, sib_left, own = {}, {}, {}, {}, {}
    for p in (0, 1):
        own[p] = moved(me, p, sib_s.at[0, p], sib_r.at[0, p], sibling, True)
    for s, p in steps:
        from_left = 2 * jnp.maximum(z - s, 0) + core
        from_right = 2 * jnp.minimum(z + s, 3) + core
        rights[s, p] = moved(
            2 * jnp.maximum(z - s + 1, 0) + core, p, right_s.at[s - 1, p], right_r.at[s - 1, p],
            right, s == 1,
        )
        lefts[s, p] = moved(
            2 * jnp.minimum(z + s - 1, 3) + core, p, left_s.at[s - 1, p], left_r.at[s - 1, p],
            left, s == 1,
        )
        sib_right[s, p] = moved(from_left, p, sib_s.at[s, p], sib_r.at[s, p], sibling, False)
        sib_left[s, p] = moved(
            from_right, p, sib_s.at[3 + s, p], sib_r.at[3 + s, p], sibling, False
        )

    def goes_right(s):
        return (z < 3) & (z >= s - 1)

    def goes_left(s):
        return (z > 0) & (z + s <= 4)

    for p in (0, 1):
        pl.when(goes_right(1))(rights[1, p].start)
        pl.when(goes_left(1))(lefts[1, p].start)
    for p in (0, 1):
        own[p].start()
    keep = pltpu.make_async_copy(x_ref, out_ref.at[me], own_s)
    keep.start()
    for s, p in steps:
        @pl.when(z >= s)
        def _():
            rights[s, p].wait_recv()
            sib_right[s, p].start()

        if s < 3:
            pl.when(goes_right(s + 1))(rights[s + 1, p].start)

        @pl.when(z + s <= 3)
        def _():
            lefts[s, p].wait_recv()
            sib_left[s, p].start()

        if s < 3:
            pl.when(goes_left(s + 1))(lefts[s + 1, p].start)
    keep.wait()
    for p in (0, 1):
        own[p].wait()
    for s, p in steps:
        pl.when(goes_right(s))(rights[s, p].wait_send)
        pl.when(goes_left(s))(lefts[s, p].wait_send)
        pl.when(z >= s)(sib_right[s, p].wait)
        pl.when(z + s <= 3)(sib_left[s, p].wait)


def line_gather(x):
    dma = pltpu.SemaphoreType.DMA
    whole = pl.BlockSpec(memory_space=pltpu.VMEM)
    return pl.pallas_call(
        gather_kernel,
        out_shape=jax.ShapeDtypeStruct((8, *x.shape), x.dtype),
        in_specs=[whole],
        out_specs=whole,
        scratch_shapes=[*[dma((3, 2)) for _ in range(4)], dma((7, 2)), dma((7, 2)), dma(())],
        compiler_params=pltpu.CompilerParams(
            collective_id=1, has_side_effects=True, vmem_limit_bytes=32 * 2**20
        ),
        name="line_gather",
    )(x)


def dot3t(a, b):
    def one(p, q):
        return lax.dot_general(p, q, (((0,), (0,)), ((), ())), preferred_element_type=F32)

    return one(a[0], b[0]) + (one(a[1], b[0]) + one(a[0], b[1]))


def partial_kernel(size, keep_ref, root_ref, all_ref, pair_ref, scaled_ref, mine_ref, chain_ref,
                   panel_ref, part_ref):
    tile = lax.axis_index("row") // 2
    panel = block = None
    for i in range(3):
        if i < 2:
            projected = None
            for b in range(4):
                term = mm(root_ref[b], all_ref[2 * b:2 * b + 2, i].reshape(size, size))
                projected = term if projected is None else projected + term
        else:
            projected = mm(root_ref[tile], pair_ref[...])
        scaled = split(scaled_ref[i])
        mine = split(mine_ref[i])
        if i:
            chain = split(chain_ref[i - 1])
            projected = projected + dot3(panel, chain)
            cross = -(dot3t(panel, scaled) + dot3(block, chain))
            part_ref[(2 + i) * size:(3 + i) * size] = cross
        kept = jnp.where(keep_ref[i] > 0, -projected, 0.0)
        panel_ref[0, i] = kept
        panel = split(kept)
        value = dot3t(mine, mine) - dot3t(scaled, panel)
        if i:
            value = value - dot3t(chain, split(cross))
        part_ref[i * size:(i + 1) * size] = value
        block = split(value)
    rest = part_ref.shape[0] - 5 * size
    part_ref[5 * size:] = jnp.zeros((rest, size), F32)


def partials(keep, root, everyone, pair, scaled, mine, chain):
    size = scaled.shape[-1]
    rows = -(-5 * size // 128) * 128
    whole = pl.BlockSpec(memory_space=pltpu.VMEM)
    return pl.pallas_call(
        functools.partial(partial_kernel, size),
        out_shape=(
            jax.ShapeDtypeStruct((1, *scaled.shape), F32),
            jax.ShapeDtypeStruct((rows, size), F32),
        ),
        in_specs=[pl.BlockSpec(memory_space=pltpu.SMEM)] + [whole] * 6,
        out_specs=(whole, whole),
        compiler_params=pltpu.CompilerParams(vmem_limit_bytes=52 * 2**20),
        name="partials",
    )(keep, root, everyone, pair, scaled, mine, chain)


def on_device(root_cov, diag_factor, panel_factor, chain_factor, panel_tiles):
    node_width = diag_factor.shape[-1]
    rows_here = panel_factor.shape[2]
    per_tile = node_width // rows_here
    row_count = lax.axis_size("row")
    tile_total = row_count // per_tile
    counts = (3 * tile_total // 4, tile_total // 2, tile_total // 4)
    small = row_count == 8 and tile_total == 4 and root_cov.shape[1] == node_width
    if small:
        root_rows = lax.all_gather(root_cov, "branch")
    else:
        root_rows = lax.all_gather(root_cov, "branch", axis=1, tiled=True)
    me = lax.axis_index("row")
    my_tile = me // per_tile
    inverse_all = inverses(diag_factor)
    share = -(-node_width // row_count // 8) * 8
    padded = jnp.pad(inverse_all, ((0, 0), (0, share * row_count - node_width), (0, 0)))
    mine = lax.dynamic_slice_in_dim(padded, me * share, share, axis=1)
    chosen = [jnp.any(panel_tiles[0, : counts[i]] == my_tile) for i in range(3)]
    scaled = [
        jnp.where(chosen[i], product(panel_factor[0, i], inverse_all[i]), 0.0) for i in range(3)
    ]
    if small:
        rounded = [x.astype(BF) for x in scaled]
        theirs = lax.ppermute(rounded[2], "row", [(d, d ^ 1) for d in range(row_count)])
        pair = jnp.where(
            me % 2 == 0,
            jnp.concatenate([rounded[2], theirs]),
            jnp.concatenate([theirs, rounded[2]]),
        )
        everyone = line_gather(jnp.stack(rounded[:2]))
        chain_all = jnp.stack([product(chain_factor[0, i - 1], inverse_all[i]) for i in (1, 2)])
        panel_out, parts = partials(
            jnp.stack(chosen).astype(jnp.int32), root_rows, everyone, pair, jnp.stack(scaled),
            mine, chain_all,
        )
        total = line_sum(parts, 5 * node_width)
        return (panel_out, total.reshape(1, 5, node_width, node_width))
    panels = []
    blocks = []
    crosses = []
    for i in range(3):
        rounded = scaled[i].astype(BF)
        gathered = jnp.dot(
            root_rows,
            lax.all_gather(rounded, "row", axis=0, tiled=True),
            preferred_element_type=F32,
        )
        left = jnp.concatenate([mine[i], scaled[i]], axis=0)
        if i == 0:
            panel = -jnp.where(chosen[i], gathered, 0.0)
            block = product(left.T, jnp.concatenate([mine[i], -panel], axis=0))
        else:
            chain = product(chain_factor[0, i - 1], inverse_all[i])
            panel = -jnp.where(chosen[i], gathered + product(panels[-1], chain), 0.0)
            cross = -(product(panels[-1].T, scaled[i]) + product(blocks[-1], chain))
            block = product(left.T, jnp.concatenate([mine[i], -panel], axis=0)) - product(
                chain.T, cross
            )
            crosses.append(cross)
        panels.append(panel)
        blocks.append(block)
    total = lax.psum(jnp.stack(blocks + crosses), "row")
    return (jnp.stack(panels)[None], total[None])


def solution(mesh):
    in_specs = (
        P("row", "branch"),
        P("branch", None, None, None),
        P("branch", None, "row", None),
        P("branch", None, None, None),
        P("branch", None),
    )
    out_specs = (P("branch", None, "row", None), P("branch", None, None, None))
    return jax.shard_map(
        on_device, mesh=mesh, in_specs=in_specs, out_specs=out_specs, check_vma=False
    )
```

profile of v0, /device:TPU:0, one launch (start us, length us, event | category | flops | bytes accessed | tf_op | source)
XLA Modules:
  0.0 239.6 jit_solution(12061691324562750237)
XLA Ops:
  7.2 0.0 all-gather.3.cloned.1.call-start
  7.2 0.7 all-gather.3.cloned.1.call-update
  7.9 0.0 copy-start.5
  7.9 17.2 %inverses.1 = f32[3,576,576]{2,1,0:T(8,128)S(1)} custom-call(f32[1,3,576,576]{3,2,1,0:T(8,128)} %l_ref.1), custom_call_target="tpu_custom_call" | custom-call | tf_op jit(solution)/shard_map/inverses/pallas_call | solution.py:83
  25.1 0.0 copy-start
  25.1 2.0 copy-done
  27.2 2.7 %fusion.24 = (bf16[288,576]{1,0:T(8,128)(2,1)S(1)}, f32[288,576]{1,0:T(8,128)S(1)}) fusion(f32[3,576,576]{2,1,0:T(8,128)} %copy-done, f32[1,3,288,576]{3,2,1,0:T(8,128)S(1)} %copy-done.4, pred[]{:T(512)} %bitcast.11), kind=kOutput, calls=%fused_computation.33 | convolution fusion | flops 573640704 | bytes 3207680 | tf_op jit(solution)/shard_map/dot_general | solution.py:15
  29.9 0.5 collective-permute-start
  30.4 0.7 compare_reduce_fusion
  31.1 3.4 %fusion.16 = f32[288,576]{1,0:T(8,128)S(1)} fusion(f32[3,576,576]{2,1,0:T(8,128)} %copy-done, f32[1,3,288,576]{3,2,1,0:T(8,128)S(1)} %copy-done.4, pred[]{:T(512)} %compare_reduce_fusion), kind=kOutput, calls=%fused_computation.17 | convolution fusion | flops 573474816 | bytes 2875904 | tf_op jit(solution)/shard_map/dot_general | solution.py:15
  34.5 0.7 compare_reduce_fusion.1
  35.3 0.0 copy-done.1
  35.3 1.9 fusion.17
  37.2 0.1 convert_bitcast_fusion
  37.3 0.1 pad_maximum_fusion.2.x_ref
  37.4 0.0 copy-start.3
  37.4 1.5 pad_maximum_fusion.1.scaled_ref
  38.9 1.1 copy-done.3
  40.1 2.2 fusion.10
  42.3 3.3 %fusion.7 = f32[1,576,576]{2,1,0:T(8,128)} fusion(f32[1,2,576,576]{3,2,1,0:T(8,128)S(1)} %copy-done.3, f32[3,576,576]{2,1,0:T(8,128)S(1)} %copy-done.1), kind=kOutput, calls=%fused_computation.12 | convolution fusion | flops 1146617856 | bytes 4276224 | tf_op jit(solution)/shard_map/dot_general | solution.py:15
  45.6 1.4 add_convert_fusion.keep_ref
  47.0 55.2 %line_gather.1.all_ref = bf16[8,2,288,576]{3,2,1,0:T(8,128)(2,1)S(1)} custom-call(bf16[2,288,576]{2,1,0:T(8,128)(2,1)S(1)} %pad_maximum_fusion.2.x_ref), custom_call_target="tpu_custom_call" | custom-call | tf_op jit(solution)/shard_map/line_gather/pallas_call | solution.py:330
  102.3 0.0 copy-start.2
  102.3 2.6 %copy-done.2 = bf16[8,2,288,576]{3,2,1,0:T(8,128)(2,1)} copy-done((bf16[8,2,288,576]{3,2,1,0:T(8,128)(2,1)}, bf16[8,2,288,576]{3,2,1,0:T(8,128)(2,1)S(1)}, u32[]{:S(2)}) %copy-start.2) | copy-done | bytes 5308440
  104.9 1.1 constant_dynamic-slice_fusion.mine_ref
  106.0 3.4 %pad_maximum_fusion.chain_ref = f32[2,576,576]{2,1,0:T(8,128)} fusion(f32[1,576,576]{2,1,0:T(8,128)S(1)} %fusion.10, f32[1,576,576]{2,1,0:T(8,128)} %fusion.7), kind=kLoop, calls=%fused_computation | loop fusion | flops 663552 | bytes 5308416 | tf_op jit(solution)/shard_map/stack | solution.py:429
  109.4 0.0 collective-permute-done
  109.4 0.3 maximum_select_fusion.pair_ref
  109.6 0.0 all-gather.3.cloned.1.call-done
  109.7 28.9 %partials.1 = (f32[1,3,288,576]{3,2,1,0:T(8,128)}, f32[2944,576]{1,0:T(8,128)}) custom-call(s32[3]{0:T(128)S(1)} %add_convert_fusion.keep_ref, bf16[4,288,576]{2,1,0:T(8,128)(2,1)} %bitcast.67, bf16[8,2,288,576]{3,2,1,0:T(8,128)(2,1)} %copy-done.2, bf16[576,576]{1,0:T(8,128)(2,1)S(1)} %maximum_select_fusion.pair_ref, ...), custom_call_target="tpu_custom_call" | custom-call | tf_op jit(solution)/shard_map/partials/pallas_call | solution.py:385
  138.6 87.6 %line_sum.1 = f32[2,4,368,576]{3,2,1,0:T(8,128)} custom-call(f32[2,4,368,576]{3,2,1,0:T(8,128)} %bitcast.62), custom_call_target="tpu_custom_call" | custom-call | tf_op jit(solution)/shard_map/line_sum/pallas_call | solution.py:224
  226.2 6.6 %slice.49 = f32[2880,576]{1,0:T(8,128)} slice(f32[2944,576]{1,0:T(8,128)} %bitcast.61), slice={[0:2880], [0:576]} | slice | bytes 13271040 | tf_op jit(solution)/shard_map/slice | solution.py:243
  (4 shorter events, 0.0 us)
Async XLA Ops:
  7.2 102.5 %all-gather.3.cloned.1.call-start = ((), (), s32[]{:S(2)}) async-start(), calls=%async_computation | async-start | bytes 1843200 | tf_op jit(solution)/shard_map/all_gather | solution.py:407
  7.9 19.2 %copy-start.5 = (s32[1,3]{1,0:T(1,128)S(1)}, s32[1,3]{1,0:T(1,128)}, u32[]{:S(2)}) copy-start(s32[1,3]{1,0:T(1,128)} %param.9) | copy-start | bytes 40
  7.9 19.2 %copy-start.4 = (f32[1,3,288,576]{3,2,1,0:T(8,128)S(1)}, f32[1,3,288,576]{3,2,1,0:T(8,128)}, u32[]{:S(2)}) copy-start(f32[1,3,288,576]{3,2,1,0:T(8,128)} %param.7) | copy-start | bytes 5971972
  25.1 2.0 copy-start
  27.2 8.1 %copy-start.1 = (f32[3,576,576]{2,1,0:T(8,128)S(1)}, f32[3,576,576]{2,1,0:T(8,128)}, u32[]{:S(2)}) copy-start(f32[3,576,576]{2,1,0:T(8,128)} %copy-done) | copy-start | bytes 11943940
  29.9 79.5 %collective-permute-start = (bf16[288,576]{1,0:T(8,128)(2,1)S(1)}, bf16[288,576]{1,0:T(8,128)(2,1)S(1)}, u32[]{:S(2)}, u32[]{:S(2)}) collective-permute-start(bf16[288,576]{1,0:T(8,128)(2,1)S(1)} %get-tuple-element.6), channel_id=1, source_target_pairs={{0,1},{1,0},{2,3},{3,2},{4,5},{5,4},{6,7},{7,6},{8,9},{9,8},{10,11... | collective-permute-start | bytes 995336 | tf_op jit(solution)/shard_map/ppermute | solution.py:422
  37.4 2.6 %copy-start.3 = (f32[1,2,576,576]{3,2,1,0:T(8,128)S(1)}, f32[1,2,576,576]{3,2,1,0:T(8,128)}, u32[]{:S(2)}) copy-start(f32[1,2,576,576]{3,2,1,0:T(8,128)} %param.8) | copy-start | bytes 7962628
  102.3 2.6 %copy-start.2 = (bf16[8,2,288,576]{3,2,1,0:T(8,128)(2,1)}, bf16[8,2,288,576]{3,2,1,0:T(8,128)(2,1)S(1)}, u32[]{:S(2)}) copy-start(bf16[8,2,288,576]{3,2,1,0:T(8,128)(2,1)S(1)} %line_gather.1.all_ref) | copy-start | bytes 15925252
Sparse Core Ops, SparseCore 0:
  9.8 32.8 all-gather.2
where the time goes:
time: 240 us
  Pallas kernels  189 us (79%)
  between operations  14.2 us (6%)
  matrix products  13.6 us (6%)
  local copies, waits for them, and re-layouts  13.4 us (6%)
  other arithmetic  8.23 us (3%)
    pallas_call x1, Pallas kernels, line_sum(): pl.pallas_call(sum_kernel, out_shape=jax.ShapeDtypeStruct((2, 4, rows, co...  87.6 us
    pallas_call x1, Pallas kernels, line_gather(): pl.pallas_call(gather_kernel, out_shape=jax.ShapeDtypeStruct((8, *x.shape...  55.2 us
    pallas_call x1, Pallas kernels, partials(): pl.pallas_call(functools.partial(partial_kernel, size), out_shape=(jax.Sh...  28.9 us
    pallas_call x1, Pallas kernels, inverses(): pl.pallas_call(functools.partial(inverse_kernel, size, size // 3), grid=(...  17.2 us
    dot_general x5, matrix products, product(): jnp.dot(left_mat, right_mat, precision=lax.Precision.HIGH, preferred_elem...  13.6 us
    slice x1, local copies, waits for them, and re-layouts, line_sum(): return out.reshape(8 * rows, columns)[:total]  6.63 us
    unnamed x12, local copies, waits for them, and re-layouts  5.7 us
  transfers between devices with their start and end apart: 2, of which 0 were waited for; matrix products, arithmetic and copies ran while one was open for 10% of the time, Pallas kernels for 30%

commit v1 on v0

--- a/solution.py
+++ b/solution.py
@@ -347,8 +347,10 @@
     return one(a[0], b[0]) + (one(a[1], b[0]) + one(a[0], b[1]))
 
 
-def partial_kernel(size, keep_ref, root_ref, all_ref, pair_ref, scaled_ref, mine_ref, chain_ref,
-                   panel_ref, part_ref):
+def partial_kernel(size, keep_ref, root_ref, all_ref, pair_ref, scaled_0, scaled_1, scaled_2,
+                   mine_ref, chain_0, chain_1, panel_ref, part_ref):
+    scaled_refs = (scaled_0, scaled_1, scaled_2)
+    chain_refs = (chain_0, chain_1)
     tile = lax.axis_index("row") // 2
     panel = block = None
     for i in range(3):
@@ -359,10 +361,10 @@
                 projected = term if projected is None else projected + term
         else:
             projected = mm(root_ref[tile], pair_ref[...])
-        scaled = split(scaled_ref[i])
+        scaled = split(scaled_refs[i][...])
         mine = split(mine_ref[i])
         if i:
-            chain = split(chain_ref[i - 1])
+            chain = split(chain_refs[i - 1][...])
             projected = projected + dot3(panel, chain)
             cross = -(dot3t(panel, scaled) + dot3(block, chain))
             part_ref[(2 + i) * size:(3 + i) * size] = cross
@@ -379,20 +381,20 @@
 
 
 def partials(keep, root, everyone, pair, scaled, mine, chain):
-    size = scaled.shape[-1]
+    size = scaled[0].shape[-1]
     rows = -(-5 * size // 128) * 128
     whole = pl.BlockSpec(memory_space=pltpu.VMEM)
     return pl.pallas_call(
         functools.partial(partial_kernel, size),
         out_shape=(
-            jax.ShapeDtypeStruct((1, *scaled.shape), F32),
+            jax.ShapeDtypeStruct((1, 3, *scaled[0].shape), F32),
             jax.ShapeDtypeStruct((rows, size), F32),
         ),
-        in_specs=[pl.BlockSpec(memory_space=pltpu.SMEM)] + [whole] * 6,
+        in_specs=[pl.BlockSpec(memory_space=pltpu.SMEM)] + [whole] * 9,
         out_specs=(whole, whole),
         compiler_params=pltpu.CompilerParams(vmem_limit_bytes=52 * 2**20),
         name="partials",
-    )(keep, root, everyone, pair, scaled, mine, chain)
+    )(keep, root, everyone, pair, *scaled, mine, *chain)
 
 
 def on_device(root_cov, diag_factor, panel_factor, chain_factor, panel_tiles):
@@ -426,9 +428,9 @@
             jnp.concatenate([theirs, rounded[2]]),
         )
         everyone = line_gather(jnp.stack(rounded[:2]))
-        chain_all = jnp.stack([product(chain_factor[0, i - 1], inverse_all[i]) for i in (1, 2)])
+        chain_all = [product(chain_factor[0, i - 1], inverse_all[i]) for i in (1, 2)]
         panel_out, parts = partials(
-            jnp.stack(chosen).astype(jnp.int32), root_rows, everyone, pair, jnp.stack(scaled),
+            jnp.stack(chosen).astype(jnp.int32), root_rows, everyone, pair, scaled,
             mine, chain_all,
         )
         total = line_sum(parts, 5 * node_width)

time: 240 us -> 241 us (level)
  matrix products: 13.6 us -> 19.6 us
  other arithmetic: 8.23 us -> 4.2 us
    dot_general x5, matrix products: 13.6 us -> 19.6 us  [product(): jnp.dot(left_mat, right_mat, precision=lax.Precision.HIGH, preferred_elem...]
    another operation x2 -> x0, other arithmetic: 4.9 us -> none  [the longest x1 3.39 us: on_device(): jnp.stack([product(chain_factor[0, i - 1], inverse_all[i]) for i in (1, 2)])]
where the time goes in v1:
time: 241 us; the launch traced here: 240 us
  Pallas kernels  189 us (78%)
  matrix products  19.6 us (8%)
  between operations  14.2 us (6%)
  local copies, waits for them, and re-layouts  12.3 us (5%)
  other arithmetic  4.2 us (2%)
    pallas_call x1, Pallas kernels, line_sum(): pl.pallas_call(sum_kernel, out_shape=jax.ShapeDtypeStruct((2, 4, rows, co...  87.5 us
    pallas_call x1, Pallas kernels, line_gather(): pl.pallas_call(gather_kernel, out_shape=jax.ShapeDtypeStruct((8, *x.shape...  55.5 us
    pallas_call x1, Pallas kernels, partials(): pl.pallas_call(functools.partial(partial_kernel, size), out_shape=(jax.Sh...  28.6 us
    dot_general x5, matrix products, product(): jnp.dot(left_mat, right_mat, precision=lax.Precision.HIGH, preferred_elem...  19.6 us
    pallas_call x1, Pallas kernels, inverses(): pl.pallas_call(functools.partial(inverse_kernel, size, size // 3), grid=(...  17 us
    slice x1, local copies, waits for them, and re-layouts, line_sum(): return out.reshape(8 * rows, columns)[:total]  6.63 us
  transfers between devices with their start and end apart: 2, of which 0 were waited for; matrix products, arithmetic and copies ran while one was open for 10% of the time, Pallas kernels for 30%

profile of v1, /device:TPU:0, one launch (start us, length us, event | category | flops | bytes accessed | tf_op | source)
XLA Modules:
  0.0 240.1 jit_solution(10763467096139552166)
XLA Ops:
  7.2 0.0 all-gather.3.cloned.1.call-start
  7.2 0.7 all-gather.3.cloned.1.call-update
  7.9 0.0 copy-start.5
  7.9 0.0 copy-start.4
  7.9 17.0 %inverses.1 = f32[3,576,576]{2,1,0:T(8,128)S(1)} custom-call(f32[1,3,576,576]{3,2,1,0:T(8,128)} %l_ref.1), custom_call_target="tpu_custom_call" | custom-call | tf_op jit(solution)/shard_map/inverses/pallas_call | solution.py:83
  24.9 0.0 copy-start
  24.9 2.0 copy-done
  26.9 0.0 copy-done.5
  27.0 0.0 copy-done.4
  27.0 3.4 %fusion.18 = (bf16[288,576]{1,0:T(8,128)(2,1)S(1)}, f32[288,576]{1,0:T(8,128)}) fusion(f32[3,576,576]{2,1,0:T(8,128)} %copy-done, f32[1,3,288,576]{3,2,1,0:T(8,128)S(1)} %copy-done.4, pred[]{:T(512)} %bitcast.11), kind=kOutput, calls=%fused_computation.29 | convolution fusion | flops 573640704 | bytes 3207680 | tf_op jit(solution)/shard_map/dot_general | solution.py:15
  30.4 0.5 collective-permute-start
  30.9 0.7 compare_reduce_fusion.1
  31.6 0.7 compare_reduce_fusion
  32.2 3.2 %fusion.10.scaled_1 = f32[288,576]{1,0:T(8,128)S(1)} fusion(f32[3,576,576]{2,1,0:T(8,128)} %copy-done, f32[1,3,288,576]{3,2,1,0:T(8,128)S(1)} %copy-done.4, pred[]{:T(512)} %compare_reduce_fusion), kind=kOutput, calls=%fused_computation.13 | convolution fusion | flops 573474816 | bytes 2875904 | tf_op jit(solution)/shard_map/dot_general | solution.py:15
  35.4 0.0 copy-start.2
  35.4 3.2 %fusion.11.scaled_0 = f32[288,576]{1,0:T(8,128)S(1)} fusion(f32[3,576,576]{2,1,0:T(8,128)} %copy-done, f32[1,3,288,576]{3,2,1,0:T(8,128)S(1)} %copy-done.4, pred[]{:T(512)} %compare_reduce_fusion.1), kind=kOutput, calls=%fused_computation.14 | convolution fusion | flops 573474816 | bytes 2875904 | tf_op jit(solution)/shard_map/dot_general | solution.py:15
  38.6 0.1 convert_bitcast_fusion
  38.7 0.1 pad_maximum_fusion.x_ref
  38.8 55.5 %line_gather.1.all_ref = bf16[8,2,288,576]{3,2,1,0:T(8,128)(2,1)S(1)} custom-call(bf16[2,288,576]{2,1,0:T(8,128)(2,1)S(1)} %pad_maximum_fusion.x_ref), custom_call_target="tpu_custom_call" | custom-call | tf_op jit(solution)/shard_map/line_gather/pallas_call | solution.py:330
  94.3 0.0 copy-start.1
  94.3 2.6 %copy-done.1 = bf16[8,2,288,576]{3,2,1,0:T(8,128)(2,1)} copy-done((bf16[8,2,288,576]{3,2,1,0:T(8,128)(2,1)}, bf16[8,2,288,576]{3,2,1,0:T(8,128)(2,1)S(1)}, u32[]{:S(2)}) %copy-start.1) | copy-done | bytes 5308440
  96.9 1.3 add_convert_fusion.keep_ref
  98.2 1.1 constant_dynamic-slice_fusion.mine_ref
  99.3 0.0 copy-start.3
  99.3 5.2 %fusion.1.chain_1 = f32[576,576]{1,0:T(8,128)} fusion(f32[1,2,576,576]{3,2,1,0:T(8,128)} %param.8, f32[3,576,576]{2,1,0:T(8,128)} %copy-done), kind=kOutput, calls=%fused_computation.4 | convolution fusion | flops 1146617856 | bytes 4276224 | tf_op jit(solution)/shard_map/dot_general | solution.py:15
  104.5 4.6 %fusion.3.chain_0 = f32[576,576]{1,0:T(8,128)} fusion(f32[1,2,576,576]{3,2,1,0:T(8,128)S(1)} %copy-done.3, f32[3,576,576]{2,1,0:T(8,128)} %copy-done), kind=kOutput, calls=%fused_computation.6 | convolution fusion | flops 1146617856 | bytes 4276224 | tf_op jit(solution)/shard_map/dot_general | solution.py:15
  109.1 0.0 collective-permute-done
  109.1 1.3 maximum_select_fusion.pair_ref
  110.5 0.0 all-gather.3.cloned.1.call-done
  110.5 28.6 %partials.1 = (f32[1,3,288,576]{3,2,1,0:T(8,128)}, f32[2944,576]{1,0:T(8,128)}) custom-call(s32[3]{0:T(128)S(1)} %add_convert_fusion.keep_ref, bf16[4,288,576]{2,1,0:T(8,128)(2,1)} %bitcast.53, bf16[8,2,288,576]{3,2,1,0:T(8,128)(2,1)} %copy-done.1, bf16[576,576]{1,0:T(8,128)(2,1)S(1)} %maximum_select_fusion.pair_ref, f32[288,576]{1,0:T(8,128)S(1)} %fusion.11.scaled_0, ...), custom_call_target="tpu_custom_call" | custom-call | tf_op jit(solution)/shard_map/partials/pallas_call | solution.py:387
  139.1 87.5 %line_sum.1 = f32[2,4,368,576]{3,2,1,0:T(8,128)} custom-call(f32[2,4,368,576]{3,2,1,0:T(8,128)} %bitcast.51), custom_call_target="tpu_custom_call" | custom-call | tf_op jit(solution)/shard_map/line_sum/pallas_call | solution.py:224
  226.6 6.6 %slice.49 = f32[2880,576]{1,0:T(8,128)} slice(f32[2944,576]{1,0:T(8,128)} %bitcast.50), slice={[0:2880], [0:576]} | slice | bytes 13271040 | tf_op jit(solution)/shard_map/slice | solution.py:243
  (2 shorter events, 0.0 us)
Async XLA Ops:
  7.2 103.3 %all-gather.3.cloned.1.call-start = ((), (), s32[]{:S(2)}) async-start(), calls=%async_computation | async-start | bytes 1843200 | tf_op jit(solution)/shard_map/all_gather | solution.py:409
  7.9 19.0 %copy-start.5 = (s32[1,3]{1,0:T(1,128)S(1)}, s32[1,3]{1,0:T(1,128)}, u32[]{:S(2)}) copy-start(s32[1,3]{1,0:T(1,128)} %param.9) | copy-start | bytes 40
  7.9 19.1 %copy-start.4 = (f32[1,3,288,576]{3,2,1,0:T(8,128)S(1)}, f32[1,3,288,576]{3,2,1,0:T(8,128)}, u32[]{:S(2)}) copy-start(f32[1,3,288,576]{3,2,1,0:T(8,128)} %param.7) | copy-start | bytes 5971972
  24.9 2.0 copy-start
  30.4 78.7 %collective-permute-start = (bf16[288,576]{1,0:T(8,128)(2,1)S(1)}, bf16[288,576]{1,0:T(8,128)(2,1)}, u32[]{:S(2)}, u32[]{:S(2)}) collective-permute-start(bf16[288,576]{1,0:T(8,128)(2,1)S(1)} %get-tuple-element.6), channel_id=1, source_target_pairs={{0,1},{1,0},{2,3},{3,2},{4,5},{5,4},{6,7},{7,6},{8,9},{9,8},{10,11... | collective-permute-start | bytes 995336 | tf_op jit(solution)/shard_map/ppermute | solution.py:424
  35.4 3.3 %copy-start.2 = (f32[288,576]{1,0:T(8,128)}, f32[288,576]{1,0:T(8,128)S(1)}, u32[]{:S(2)}) copy-start(f32[288,576]{1,0:T(8,128)S(1)} %fusion.10.scaled_1) | copy-start | bytes 1990660
  94.3 2.6 %copy-start.1 = (bf16[8,2,288,576]{3,2,1,0:T(8,128)(2,1)}, bf16[8,2,288,576]{3,2,1,0:T(8,128)(2,1)S(1)}, u32[]{:S(2)}) copy-start(bf16[8,2,288,576]{3,2,1,0:T(8,128)(2,1)S(1)} %line_gather.1.all_ref) | copy-start | bytes 15925252
  99.3 5.2 %copy-start.3 = (f32[1,2,576,576]{3,2,1,0:T(8,128)S(1)}, f32[1,2,576,576]{3,2,1,0:T(8,128)}, u32[]{:S(2)}) copy-start(f32[1,2,576,576]{3,2,1,0:T(8,128)} %param.8) | copy-start | bytes 7962628
Sparse Core Ops, SparseCore 0:
  9.8 32.8 all-gather.2
